TPU v7x, 32 devices: a whole 2x2x4 slice. The times are simulated.
32 devices in a mesh: loop: 4 (over x, core), group: 8 (over z, y).
Axes of the slice: x: 2, y: 2, z: 4, core: 2. Of those that a mesh axis runs over, the one named last changes fastest.
Arguments:
- picture_vectors: bfloat16 [4096, 1152], P(('loop', 'group')), may hold values from -2 to 2
- caption_vectors: bfloat16 [4096, 1152], P(('loop', 'group')), may hold values from -2 to 2
- occupied_slot_tally: int32 [32], replicated, may hold values from 0 to 128, as said below
- sharpness_array: float32 [1], replicated, may hold values from 8 to 12
- offset_shift: float32 [1], replicated, may hold values from -6 to -3
Outputs:
- image_grads: bfloat16 [4096, 1152], P(('loop', 'group'))
- text_grads: bfloat16 [4096, 1152], P(('loop', 'group'))
Inputs may be any that keep to these rules, and one draw needn't show every extreme that they name: Each entry is 0, 64 or 128; for every even device index k, occupied_slot_tally[k] + occupied_slot_tally[k + 1] = 128, and some device has 128.
All inputs are finite; a program needn't handle non-finite values.
Results may differ from a plain program's by a relative error of at most 0.0043.
Values may be sent and summed in bfloat16 or wider, within the bound.
A program may use at most 128 MiB of HBM per device.

v0:
```python
import jax
import jax.numpy as jnp
from jax import lax
from jax.sharding import PartitionSpec as P


def from_behind(value, axis, steps):
    count = lax.axis_size(axis)
    pairs = [(source, (source + steps) % count) for source in range(count)]
    return lax.ppermute(value, axis, pairs)


def unit_normalize(raw):
    values = raw.astype(jnp.float32)
    inverse = lax.rsqrt(jnp.sum(values * values, axis=1, keepdims=True) + 1e-06)
    return (values * inverse, inverse)


def project(unit, inverse, grads):
    return ((grads - unit * jnp.sum(unit * grads, axis=1, keepdims=True)) * inverse).astype(
        jnp.bfloat16
    )


def slot_rows(source, rows, kept, occupied_slot_tally):
    offsets = jnp.arange(kept, dtype=jnp.int32)
    return (source * rows + offsets, (offsets < occupied_slot_tally[source]).astype(jnp.float32))


def per_device(
    picture_vectors, caption_vectors, occupied_slot_tally, sharpness_array, offset_shift
):
    loops = lax.axis_size("loop")
    groups = lax.axis_size("group")
    rows, width = picture_vectors.shape
    here_loop = lax.axis_index("loop")
    here_group = lax.axis_index("group")
    sharpness_factor = sharpness_array[0]
    offset = offset_shift[0]
    img_unit, img_inv = unit_normalize(picture_vectors)
    txt_unit, text_inverse_norm = unit_normalize(caption_vectors)
    img_half = img_unit.astype(jnp.bfloat16)
    text_block = lax.all_gather(txt_unit.astype(jnp.bfloat16), "group", axis=0, tiled=True)
    rows_per_block = rows * groups
    text_position = jnp.arange(rows_per_block, dtype=jnp.int32)
    text_ids = here_loop * rows_per_block + text_position
    block_counts = lax.dynamic_slice_in_dim(occupied_slot_tally, here_loop * groups, groups)
    text_live = (text_position % rows < jnp.repeat(block_counts, rows)).astype(jnp.float32)
    kept = img_half.shape[0]

    def pass_grads(partial_value):
        return from_behind(partial_value, "loop", 1)

    block = img_half
    partial_value = jnp.zeros((kept, width), jnp.float32)
    accum = jnp.zeros((rows_per_block, width), jnp.float32)
    for step in range(loops):
        if step > 0:
            block = from_behind(block, "loop", 1)
            partial_value = pass_grads(partial_value)
        source = (here_loop - step) % loops * groups + here_group
        ids, live = slot_rows(source, rows, kept, occupied_slot_tally)
        logits = (
            lax.dot_general(
                block, text_block, (((1,), (1,)), ((), ())), preferred_element_type=jnp.float32
            )
            * sharpness_factor
            + offset
        )
        target = (ids[:, None] == text_ids[None, :]).astype(jnp.float32)
        weight = (
            sharpness_factor
            * live[:, None]
            * text_live[None, :]
            * (jax.nn.sigmoid(logits) - target)
        ).astype(jnp.bfloat16)
        partial_value = partial_value + jnp.dot(
            weight, text_block, preferred_element_type=jnp.float32
        )
        accum = accum + lax.dot_general(
            weight, block, (((0,), (0,)), ((), ())), preferred_element_type=jnp.float32
        )
    own_grads = pass_grads(partial_value)
    text_sum = lax.psum_scatter(accum, "group", scatter_dimension=0, tiled=True)
    return (project(img_unit, img_inv, own_grads), project(txt_unit, text_inverse_norm, text_sum))


def solution(mesh):
    return jax.shard_map(
        per_device,
        mesh=mesh,
        in_specs=(P(("loop", "group"), None), P(("loop", "group"), None), P(), P(), P()),
        out_specs=(P(("loop", "group"), None), P(("loop", "group"), None)),
        check_vma=False,
    )
```

profile of v0, /device:TPU:0, one launch (start us, length us, event | category | flops | bytes accessed | tf_op | source)
XLA Modules:
  0.0 185.4 jit_solution(16801033219787590916)
XLA Ops:
  7.2 0.0 all-gather.2.cloned.1.call-start
  7.2 1.1 fusion.47
  8.3 1.8 fusion.34
  10.1 0.0 all-gather.2.cloned.1.call-update
  10.1 0.0 reduce-scatter.2.cloned.1.call-start
  10.2 1.1 fusion.42
  11.3 1.1 fusion.37
  12.4 0.5 collective-permute-start.1
  14.2 0.7 dynamic_slice.16
  14.9 1.5 fusion.53
  16.4 0.7 compare_select_fusion
  17.1 0.6 compare_select_fusion.2
  17.7 0.6 compare_select_fusion.3
  18.3 0.9 collective-permute-done.1
  19.2 1.8 collective-permute-start.3
  21.0 0.6 compare_select_fusion.1
  21.6 0.1 fusion.52
  21.6 3.8 %collective-permute-done.3 = bf16[128,1152]{1,0:T(8,128)(2,1)} collective-permute-done((bf16[128,1152]{1,0:T(8,128)(2,1)S(1)}, bf16[128,1152]{1,0:T(8,128)(2,1)}, u32[]{:S(2)}, u32[]{:S(2)}) %collective-permute-start.3) | collective-permute-done | bytes 294944 | tf_op jit(solution)/shard_map/ppermute | solution.py:10
  25.5 40.1 %all-gather.2.cloned.1.call-done = bf16[1024,1152]{1,0:T(8,128)(2,1)} async-done(((bf16[128,1152]{1,0:T(8,128)(2,1)}), bf16[1024,1152]{1,0:T(8,128)(2,1)}) %all-gather.2.cloned.1.call-update) | async-done | bytes 2359312 | tf_op jit(solution)/shard_map/all_gather | solution.py:43
  65.6 2.6 %fusion.28 = bf16[128,1024]{1,0:T(8,128)(2,1)S(1)} fusion(bf16[128,1152]{1,0:T(8,128)(2,1)S(1)} %fusion.37, bf16[1024,1152]{1,0:T(8,128)(2,1)} %all-gather.2.cloned.1.call-done, s32[1024]{0:T(1024)S(1)} %iota_add_fusion, f32[]{:T(128)} %bitcast.42, f32[]{:T(128)} %bitcast.35, f32[1024]{0:T(1024)S(1)} %fusion.52, f32[128]{0:T(128)S(1)} %compare_select_fusion.3, ...), kind=kOutput, calls=%fused_computation.36 | convolution fusion | flops 303431680 | bytes 2925576 | tf_op jit(solution)/shard_map/dot_general | solution.py:64
  68.2 0.8 fusion.57
  69.0 0.8 copy-done
  69.9 1.0 fusion.29
  70.8 0.8 convolution_add_fusion.2
  71.6 1.9 %fusion.30 = bf16[128,1024]{1,0:T(8,128)(2,1)S(1)} fusion(bf16[128,1152]{1,0:T(8,128)(2,1)} %collective-permute-done.3, bf16[1024,1152]{1,0:T(8,128)(2,1)S(1)} %copy-done, f32[128]{0:T(128)S(1)} %compare_select_fusion.1, s32[1024]{0:T(1024)S(1)} %iota_add_fusion, f32[]{:T(128)} %bitcast.44, f32[]{:T(128)} %bitcast.37, f32[1024]{0:T(1024)S(1)} %fusion.52, ...), kind=kOutput, calls=%fused_computation.38 | convolution fusion | flops 303431680 | bytes 2925576 | tf_op jit(solution)/shard_map/dot_general | solution.py:64
  73.6 1.8 convolution_add_fusion.1
  75.4 1.9 %fusion.31 = bf16[128,1024]{1,0:T(8,128)(2,1)S(1)} fusion(bf16[128,1152]{1,0:T(8,128)(2,1)} %collective-permute-done.5, bf16[1024,1152]{1,0:T(8,128)(2,1)S(1)} %copy-done, f32[128]{0:T(128)S(1)} %compare_select_fusion, s32[1024]{0:T(1024)S(1)} %iota_add_fusion, f32[]{:T(128)} %bitcast.43, f32[]{:T(128)} %bitcast.36, f32[1024]{0:T(1024)S(1)} %fusion.52, ...), kind=kOutput, calls=%fused_computation.39 | convolution fusion | flops 303431680 | bytes 2925576 | tf_op jit(solution)/shard_map/dot_general | solution.py:64
  77.3 3.9 %convolution_add_fusion = f32[1024,1152]{1,0:T(8,128)} fusion(f32[1024,1152]{1,0:T(8,128)S(1)} %convolution_add_fusion.1, bf16[128,1024]{1,0:T(8,128)(2,1)S(1)} %fusion.31, bf16[128,1152]{1,0:T(8,128)(2,1)} %collective-permute-done.5), kind=kOutput, calls=%fused_computation | convolution fusion | flops 303169536 | bytes 9994240 | tf_op jit(solution)/shard_map/dot_general | solution.py:80
  81.2 0.0 reduce-scatter.2.cloned.1.call-update
  81.2 0.5 fusion.54
  81.7 0.1 collective-permute-start
  81.8 9.3 %collective-permute-done = f32[128,1152]{1,0:T(8,128)S(1)} collective-permute-done((f32[128,1152]{1,0:T(8,128)S(1)}, f32[128,1152]{1,0:T(8,128)S(1)}, u32[]{:S(2)}, u32[]{:S(2)}) %collective-permute-start) | collective-permute-done | bytes 589856 | tf_op jit(solution)/shard_map/ppermute | solution.py:10
  91.1 0.5 convolution_add_fusion.3
  91.6 0.1 collective-permute-start.2
  91.7 0.5 fusion.55
  92.2 8.8 %collective-permute-done.2 = f32[128,1152]{1,0:T(8,128)S(1)} collective-permute-done((f32[128,1152]{1,0:T(8,128)S(1)}, f32[128,1152]{1,0:T(8,128)S(1)}, u32[]{:S(2)}, u32[]{:S(2)}) %collective-permute-start.2) | collective-permute-done | bytes 589856 | tf_op jit(solution)/shard_map/ppermute | solution.py:10
  101.0 0.1 add.198
  101.1 0.1 collective-permute-start.4
  101.1 0.5 fusion.56
  101.7 8.8 %collective-permute-done.4 = f32[128,1152]{1,0:T(8,128)S(1)} collective-permute-done((f32[128,1152]{1,0:T(8,128)S(1)}, f32[128,1152]{1,0:T(8,128)S(1)}, u32[]{:S(2)}, u32[]{:S(2)}) %collective-permute-start.4) | collective-permute-done | bytes 589856 | tf_op jit(solution)/shard_map/ppermute | solution.py:10
  110.4 0.1 add.206
  110.5 0.1 collective-permute-start.6
  110.5 9.3 %collective-permute-done.6 = f32[128,1152]{1,0:T(8,128)S(1)} collective-permute-done((f32[128,1152]{1,0:T(8,128)S(1)}, f32[128,1152]{1,0:T(8,128)S(1)}, u32[]{:S(2)}, u32[]{:S(2)}) %collective-permute-start.6) | collective-permute-done | bytes 589856 | tf_op jit(solution)/shard_map/ppermute | solution.py:10
  119.8 0.2 fusion.38
  120.1 0.9 fusion.41
  121.0 54.3 %reduce-scatter.2.cloned.1.call-done = f32[128,1152]{1,0:T(8,128)} async-done(((f32[1024,1152]{1,0:T(8,128)}), f32[128,1152]{1,0:T(8,128)}) %reduce-scatter.2.cloned.1.call-update) | async-done | bytes 589840 | tf_op jit(solution)/shard_map/reduce_scatter | solution.py:84
  175.3 1.3 fusion.43
  176.6 2.0 %fusion.46 = bf16[128,1152]{1,0:T(8,128)(2,1)} fusion(f32[128,1152]{1,0:T(8,128)} %reduce-scatter.2.cloned.1.call-done, bf16[128,1152]{1,0:T(8,128)(2,1)S(1)} %copy-done.2, f32[128]{0:T(128)S(1)} %fusion.43, f32[128]{0:T(128)S(1)} %add_rsqrt_fusion), kind=kLoop, calls=%fused_computation.58 | loop fusion | flops 884736 | bytes 1180672 | tf_op jit(solution)/shard_map/convert_element_type | solution.py:20
  (18 shorter events, 0.1 us)
Async XLA Ops:
  7.2 58.4 %all-gather.2.cloned.1.call-start = ((), (), s32[]{:S(2)}) async-start(), calls=%async_computation.1 | async-start | bytes 2654208 | tf_op jit(solution)/shard_map/all_gather | solution.py:43
  10.1 165.1 %reduce-scatter.2.cloned.1.call-start = ((), (), s32[]{:S(2)}) async-start(), calls=%async_computation.2 | async-start | bytes 5308416 | tf_op jit(solution)/shard_map/reduce_scatter | solution.py:84
  12.4 6.8 %collective-permute-start.1 = (bf16[128,1152]{1,0:T(8,128)(2,1)S(1)}, bf16[128,1152]{1,0:T(8,128)(2,1)S(1)}, u32[]{:S(2)}, u32[]{:S(2)}) collective-permute-start(bf16[128,1152]{1,0:T(8,128)(2,1)S(1)} %fusion.37), channel_id=1, source_target_pairs={{0,8},{8,16},{16,24},{24,0},{1,9},{9,17},{17,25},{25,1},{2,10},{10... | collective-permute-start | bytes 884744 | tf_op jit(solution)/shard_map/ppermute | solution.py:10
  19.2 46.3 %copy-start.3 = (bf16[128,1152]{1,0:T(8,128)(2,1)}, bf16[128,1152]{1,0:T(8,128)(2,1)S(1)}, u32[]{:S(2)}) copy-start(bf16[128,1152]{1,0:T(8,128)(2,1)S(1)} %collective-permute-done.1) | copy-start | bytes 884740
  19.2 6.3 %collective-permute-start.3 = (bf16[128,1152]{1,0:T(8,128)(2,1)S(1)}, bf16[128,1152]{1,0:T(8,128)(2,1)}, u32[]{:S(2)}, u32[]{:S(2)}) collective-permute-start(bf16[128,1152]{1,0:T(8,128)(2,1)S(1)} %collective-permute-done.1), channel_id=1, source_target_pairs={{0,8},{8,16},{16,24},{24,0},{1,9},{9,17},{17,25},{25,1},{2,10},{10... | collective-permute-start | bytes 884744 | tf_op jit(solution)/shard_map/ppermute | solution.py:10
  25.5 49.9 %collective-permute-start.5 = (bf16[128,1152]{1,0:T(8,128)(2,1)}, bf16[128,1152]{1,0:T(8,128)(2,1)}, u32[]{:S(2)}, u32[]{:S(2)}) collective-permute-start(bf16[128,1152]{1,0:T(8,128)(2,1)} %collective-permute-done.3), channel_id=1, source_target_pairs={{0,8},{8,16},{16,24},{24,0},{1,9},{9,17},{17,25},{25,1},{2,10},{10... | collective-permute-start | bytes 884744 | tf_op jit(solution)/shard_map/ppermute | solution.py:10
  68.2 1.7 copy-start
  68.2 1.7 copy-start.4
  81.7 9.4 %collective-permute-start = (f32[128,1152]{1,0:T(8,128)S(1)}, f32[128,1152]{1,0:T(8,128)S(1)}, u32[]{:S(2)}, u32[]{:S(2)}) collective-permute-start(f32[128,1152]{1,0:T(8,128)S(1)} %fusion.54), channel_id=1, source_target_pairs={{0,8},{8,16},{16,24},{24,0},{1,9},{9,17},{17,25},{25,1},{2,10},{10... | collective-permute-start | bytes 1769480 | tf_op jit(solution)/shard_map/ppermute | solution.py:10
  91.6 9.4 %collective-permute-start.2 = (f32[128,1152]{1,0:T(8,128)S(1)}, f32[128,1152]{1,0:T(8,128)S(1)}, u32[]{:S(2)}, u32[]{:S(2)}) collective-permute-start(f32[128,1152]{1,0:T(8,128)S(1)} %convolution_add_fusion.3), channel_id=1, source_target_pairs={{0,8},{8,16},{16,24},{24,0},{1,9},{9,17},{17,25},{25,1},{2,10},{10... | collective-permute-start | bytes 1769480 | tf_op jit(solution)/shard_map/ppermute | solution.py:10
  101.0 18.8 %copy-start.1 = (bf16[128,1152]{1,0:T(8,128)(2,1)S(1)}, bf16[128,1152]{1,0:T(8,128)(2,1)}, u32[]{:S(2)}) copy-start(bf16[128,1152]{1,0:T(8,128)(2,1)} %param.5) | copy-start | bytes 884740
  101.1 9.4 %collective-permute-start.4 = (f32[128,1152]{1,0:T(8,128)S(1)}, f32[128,1152]{1,0:T(8,128)S(1)}, u32[]{:S(2)}, u32[]{:S(2)}) collective-permute-start(f32[128,1152]{1,0:T(8,128)S(1)} %add.198), channel_id=1, source_target_pairs={{0,8},{8,16},{16,24},{24,0},{1,9},{9,17},{17,25},{25,1},{2,10},{10... | collective-permute-start | bytes 1769480 | tf_op jit(solution)/shard_map/ppermute | solution.py:10
  101.6 73.6 %copy-start.2 = (bf16[128,1152]{1,0:T(8,128)(2,1)S(1)}, bf16[128,1152]{1,0:T(8,128)(2,1)}, u32[]{:S(2)}) copy-start(bf16[128,1152]{1,0:T(8,128)(2,1)} %param.6) | copy-start | bytes 884740
  110.5 9.4 %collective-permute-start.6 = (f32[128,1152]{1,0:T(8,128)S(1)}, f32[128,1152]{1,0:T(8,128)S(1)}, u32[]{:S(2)}, u32[]{:S(2)}) collective-permute-start(f32[128,1152]{1,0:T(8,128)S(1)} %add.206), channel_id=1, source_target_pairs={{0,8},{8,16},{16,24},{24,0},{1,9},{9,17},{17,25},{25,1},{2,10},{10... | collective-permute-start | bytes 1769480 | tf_op jit(solution)/shard_map/ppermute | solution.py:10
Sparse Core Ops, SparseCore 0:
  10.8 54.7 all-gather.1
  81.3 93.9 reduce-scatter.1
where the time goes:
time: 186 us; the launch traced here: 185 us
  waiting for transfers between devices  135 us (73%)
  matrix products  16.8 us (9%)
  between operations  15.6 us (8%)
  other arithmetic  12.2 us (7%)
  local copies, waits for them, and re-layouts  3.06 us (2%)
  starting transfers between devices  2.57 us (1%)
    reduce_scatter x1, waiting for transfers between devices, per_device(): text_sum = lax.psum_scatter(accum, 'group', scatter_dimension=0, tiled=True)  54.3 us
    ppermute x7, waiting for transfers between devices, from_behind(): return lax.ppermute(value, axis, pairs)  40.9 us
    all_gather x1, waiting for transfers between devices, per_device(): lax.all_gather(txt_unit.astype(jnp.bfloat16), 'group', axis=0, tiled=True)  40.1 us
    dot_general x4, matrix products, per_device(): lax.dot_general(block, text_block, (((1,), (1,)), ((), ())), preferred_el...  7.4 us
    dot_general x4, matrix products, per_device(): lax.dot_general(weight, block, (((0,), (0,)), ((), ())), preferred_elemen...  7.28 us
  transfers between devices with their start and end apart: 9, of which 8 were waited for; matrix products, arithmetic and copies ran while one was open for 10% of the time, Pallas kernels for 0%

commit v1 on v0

v1 whole, which is shorter than its diff:
```python
import functools

import jax
import jax.numpy as jnp
from jax import lax
from jax.experimental import pallas as pl
from jax.experimental.pallas import tpu as pltpu
from jax.sharding import PartitionSpec as P

MESH = pl.DeviceIdType.MESH
F32 = jnp.float32
BF16 = jnp.bfloat16


def unit_normalize(raw):
    values = raw.astype(F32)
    inverse = lax.rsqrt(jnp.sum(values * values, axis=1, keepdims=True) + 1e-06)
    return values * inverse, inverse


def project(raw, grads):
    unit, inverse = unit_normalize(raw)
    radial = jnp.sum(unit * grads, axis=1, keepdims=True)
    return ((grads - unit * radial) * inverse).astype(BF16)


def kernel(
    far,
    img_ref,
    txt_ref,
    tally_ref,
    sharp_ref,
    shift_ref,
    img_out,
    txt_out,
    images,
    pair_in,
    pair_own,
    texts,
    weights,
    img_send,
    img_recv,
    img_keep,
    img_send2,
    img_recv2,
    core_send,
    core_recv,
    txt_keep,
    txt_send,
    txt_recv,
    txt_send2,
    txt_recv2,
    last_send,
    last_recv,
    send_sem,
    recv_sem,
):
    rows, width = img_ref.shape
    half = rows // 2
    loop = lax.axis_index("loop")
    group = lax.axis_index("group")
    x, core = loop // 2, loop % 2
    h, z, y = group // 4, (group // 2) % 2, group % 2

    x_peer = (2 * (1 - x) + core, group)
    core_peer = (2 * x + 1 - core, group)
    z_peer = (loop, 4 * h + 2 * (1 - z) + y)
    y_peer = (loop, 4 * h + 2 * z + 1 - y)

    def h_peer(j):
        return (loop, 4 * ((h + j) % far) + 2 * z + y)

    barrier = pltpu.get_barrier_semaphore()
    peers = [x_peer, core_peer, z_peer, y_peer] + [h_peer(j) for j in range(1, far)]
    for peer in peers:
        pl.semaphore_signal(barrier, inc=1, device_id=peer, device_id_type=MESH)

    started = []

    def remote(index, src, dst, peer):
        return pltpu.make_async_remote_copy(
            src_ref=src,
            dst_ref=dst,
            send_sem=send_sem.at[index],
            recv_sem=recv_sem.at[index],
            device_id=peer,
            device_id_type=MESH,
        )

    def start(index, src, dst, peer):
        copy = remote(index, src, dst, peer)
        copy.start()
        started.append(copy)
        return copy

    own = 2 * x + z
    beside = 2 * x + 1 - z
    txt_unit, _ = unit_normalize(txt_ref[...])
    pair_own[...] = txt_unit.astype(BF16)
    pl.semaphore_wait(barrier, len(peers))
    pair_copy = start(0, pair_own, pair_in, y_peer)
    img_unit, _ = unit_normalize(img_ref[...])
    images[own] = img_unit.astype(BF16)
    z_copy = start(1, images.at[own], images.at[own], z_peer)
    x_copy = start(2, images.at[own], images.at[own], x_peer)

    device = loop * (4 * far) + group
    tally_own = tally_ref[device]
    tally_peer = tally_ref[loop * (4 * far) + 4 * h + 2 * z + 1 - y]
    has_own = jnp.minimum(tally_own, 1).astype(F32)
    has_peer = jnp.minimum(tally_peer, 1).astype(F32)

    pair_copy.wait_recv()
    texts[core, h, y] = (
        pair_own[:half].astype(F32) * has_own + pair_in[half:].astype(F32) * (1.0 - has_own)
    ).astype(BF16)
    far_copies = []
    for j in range(1, far):
        far_copies.append(start(10 + j, texts.at[core, h, y], texts.at[core, h, y], h_peer(j)))
    texts[core, h, 1 - y] = (
        pair_in[:half].astype(F32) * has_peer + pair_own[half:].astype(F32) * (1.0 - has_peer)
    ).astype(BF16)
    core_copies = [start(3, texts.at[core, h], texts.at[core, h], core_peer)]

    z_copy.wait_recv()
    x_forward = start(4, images.at[beside], images.at[beside], x_peer)

    y_forwards = []
    for j in range(1, far):
        source = (h + far - j) % far
        far_copies[j - 1].wait_recv()
        slot = texts.at[core, source, y]
        y_forwards.append(start(10 + far + j, slot, slot, y_peer))
    for j in range(1, far):
        source = (h + far - j) % far
        y_forwards[j - 1].wait_recv()
        both = texts.at[core, source]
        core_copies.append(start(10 + 2 * far + j, both, both, core_peer))
    for copy in core_copies:
        copy.wait_recv()

    sharpness = sharp_ref[0]
    shift = shift_ref[0]
    row_ids = lax.broadcasted_iota(jnp.int32, (rows, 1), 0)

    def text_block(c):
        return texts[c].reshape(far * rows, width)

    def image_step(sx, sz):
        place = 2 * sx + sz
        block = images[place]
        tally = tally_ref[(2 * sx + core) * (4 * far) + 4 * h + 2 * sz + y]
        scale = jnp.where(row_ids < tally, sharpness, 0.0)
        total = None
        for c in range(2):
            block_texts = text_block(c)
            logits = (
                lax.dot_general(
                    block, block_texts, (((1,), (1,)), ((), ())), preferred_element_type=F32
                )
                * sharpness
                + shift
            )
            pulled = 1.0 / (1.0 + jnp.exp(-logits))
            if sx is x and sz is z:
                base = h * rows
                near = base + y * half + row_ids
                later = base + (1 - y) * half + row_ids - half
                goal = jnp.where(row_ids < half, near, later)
                goal = jnp.where(core == c, goal, -1)
                columns = lax.broadcasted_iota(jnp.int32, logits.shape, 1)
                pulled = pulled - jnp.where(columns == goal, 1.0, 0.0)
            weight = (scale * pulled).astype(BF16)
            weights[c, pl.ds(pl.multiple_of(place * rows, rows), rows)] = weight
            term = jnp.dot(weight, block_texts, preferred_element_type=F32)
            total = term if total is None else total + term
        return total

    x_copy.wait_recv()
    img_send[z] = image_step(1 - x, z).astype(BF16)
    img_first = start(5, img_send.at[z], img_recv.at[z], x_peer)
    x_forward.wait_recv()
    other_z = 1 - z
    img_send[other_z] = image_step(1 - x, other_z).astype(BF16)
    img_second = start(6, img_send.at[other_z], img_recv.at[other_z], x_peer)
    img_keep[other_z] = image_step(x, other_z)
    img_keep[z] = image_step(x, z)

    all_images = images[...].reshape(4 * rows, width)

    def text_grads(c):
        return lax.dot_general(
            weights[c], all_images, (((0,), (0,)), ((), ())), preferred_element_type=F32
        )

    core_send[...] = text_grads(1 - core)
    core_copy = start(7, core_send, core_recv, core_peer)
    txt_keep[...] = text_grads(core).reshape(far, 2, half, width)

    core_copy.wait_recv()
    merged = core_recv.reshape(far, 2, half, width)
    for p in range(far):
        txt_send[p] = (txt_keep[p, 1 - y] + merged[p, 1 - y]).astype(BF16)
    y_copy = start(8, txt_send, txt_recv, y_peer)

    img_second_slot = other_z
    img_first.wait_recv()
    img_second.wait_recv()
    img_send2[...] = (img_keep[img_second_slot] + img_recv[img_second_slot].astype(F32)).astype(BF16)
    img_last = start(9, img_send2, img_recv2, z_peer)

    y_copy.wait_recv()
    back = []
    for j in range(1, far):
        goal_h = (h + j) % far
        txt_send2[j] = (
            txt_keep[goal_h, y] + merged[goal_h, y] + txt_recv[goal_h].astype(F32)
        ).astype(BF16)
        back.append(start(10 + 3 * far + j, txt_send2.at[j], txt_recv2.at[j], h_peer(j)))
    slot_sum = txt_keep[h, y] + merged[h, y] + txt_recv[h].astype(F32)

    img_last.wait_recv()
    img_sum = img_keep[z] + img_recv[z].astype(F32) + img_recv2[...].astype(F32)
    img_out[...] = project(img_ref[...], img_sum)

    for j in range(1, far):
        back[j - 1].wait_recv()
        slot_sum = slot_sum + txt_recv2[j].astype(F32)
    last_send[...] = slot_sum.astype(BF16)
    last_copy = start(10, last_send, last_recv, y_peer)
    txt_out[:half] = project(txt_ref[:half], slot_sum * has_own)
    last_copy.wait_recv()
    txt_out[half:] = project(txt_ref[half:], last_recv[...].astype(F32) * (1.0 - has_peer))

    for copy in started:
        copy.wait_send()


def per_device(far, pictures, captions, tally, sharpness, shift):
    rows, width = pictures.shape
    half = rows // 2
    vmem = pl.BlockSpec(memory_space=pltpu.VMEM)
    smem = pl.BlockSpec(memory_space=pltpu.SMEM)
    shape = jax.ShapeDtypeStruct((rows, width), BF16)
    copies = 10 + 4 * far
    return pl.pallas_call(
        functools.partial(kernel, far),
        out_shape=(shape, shape),
        in_specs=[vmem, vmem, smem, smem, smem],
        out_specs=(vmem, vmem),
        scratch_shapes=[
            pltpu.VMEM((4, rows, width), BF16),
            pltpu.VMEM((rows, width), BF16),
            pltpu.VMEM((rows, width), BF16),
            pltpu.VMEM((2, far, 2, half, width), BF16),
            pltpu.VMEM((2, 4 * rows, far * rows), BF16),
            pltpu.VMEM((2, rows, width), BF16),
            pltpu.VMEM((2, rows, width), BF16),
            pltpu.VMEM((2, rows, width), F32),
            pltpu.VMEM((rows, width), BF16),
            pltpu.VMEM((rows, width), BF16),
            pltpu.VMEM((far * rows, width), F32),
            pltpu.VMEM((far * rows, width), F32),
            pltpu.VMEM((far, 2, half, width), F32),
            pltpu.VMEM((far, half, width), BF16),
            pltpu.VMEM((far, half, width), BF16),
            pltpu.VMEM((far, half, width), BF16),
            pltpu.VMEM((far, half, width), BF16),
            pltpu.VMEM((half, width), BF16),
            pltpu.VMEM((half, width), BF16),
            pltpu.SemaphoreType.DMA((copies,)),
            pltpu.SemaphoreType.DMA((copies,)),
        ],
        compiler_params=pltpu.CompilerParams(
            collective_id=0, has_side_effects=True, vmem_limit_bytes=60 * 1024 * 1024
        ),
    )(pictures, captions, tally, sharpness, shift)


def solution(mesh):
    far = mesh.shape["group"] // 4
    spec = P(("loop", "group"), None)
    return jax.shard_map(
        functools.partial(per_device, far),
        mesh=mesh,
        in_specs=(spec, spec, P(), P(), P()),
        out_specs=(spec, spec),
        check_vma=False,
    )
```

time: 186 us -> 64.3 us (0.35)
  the two profiles are of different devices: /device:TPU:0 before, /device:TPU:8 now
where the time goes in v1:
time: 64.3 us; the launch traced here: 64.2 us
  Pallas kernels  59.8 us (93%)
  local copies, waits for them, and re-layouts  2.46 us (4%)
  between operations  1.94 us (3%)
    pallas_call x1, Pallas kernels, per_device(): pl.pallas_call(functools.partial(kernel, far), out_shape=(shape, shape),...  59.8 us
    unnamed x4, local copies, waits for them, and re-layouts  2.46 us

profile of v1, /device:TPU:8, one launch (start us, length us, event | category | flops | bytes accessed | tf_op | source)
XLA Modules:
  0.0 64.2 jit_solution(1587349219062361654)
XLA Ops:
  1.9 59.8 %shard_map.68 = (bf16[128,1152]{1,0:T(8,128)(2,1)}, bf16[128,1152]{1,0:T(8,128)(2,1)}) custom-call(bf16[128,1152]{1,0:T(8,128)(2,1)} %img_ref.1, bf16[128,1152]{1,0:T(8,128)(2,1)} %txt_ref.1, s32[32]{0:T(128)} %tally_ref.1, f32[1]{0:T(128)S(6)} %copy.9.sharp_ref, f32[1]{0:T(128)S(6)} %copy.10.shift_ref), custom_call_target="tpu_custom_call" | custom-call | tf_op jit(solution)/shard_map/pallas_call | solution.py:246
  61.7 0.0 copy-start
  61.7 1.7 %copy.11 = bf16[128,1152]{1,0:T(8,128)(2,1)} copy(bf16[128,1152]{1,0:T(8,128)(2,1)} %get-tuple-element.4) | data formatting | bytes 589824
  63.5 0.0 copy-done
  63.5 0.7 %copy.12 = bf16[128,1152]{1,0:T(8,128)(2,1)} copy(bf16[128,1152]{1,0:T(8,128)(2,1)S(1)} %copy-done) | data formatting | bytes 589824
Async XLA Ops:
  61.7 1.8 %copy-start = (bf16[128,1152]{1,0:T(8,128)(2,1)S(1)}, bf16[128,1152]{1,0:T(8,128)(2,1)}, u32[]{:S(2)}) copy-start(bf16[128,1152]{1,0:T(8,128)(2,1)} %get-tuple-element.5) | copy-start | bytes 884740

commit v2 on v1

v2 whole, which is shorter than its diff:
```python
import functools

import jax
import jax.numpy as jnp
from jax import lax
from jax.experimental import pallas as pl
from jax.experimental.pallas import tpu as pltpu
from jax.sharding import PartitionSpec as P

MESH = pl.DeviceIdType.MESH
F32 = jnp.float32
BF16 = jnp.bfloat16
PIECES = 2


def unit_normalize(raw):
    values = raw.astype(F32)
    inverse = lax.rsqrt(jnp.sum(values * values, axis=1, keepdims=True) + 1e-06)
    return values * inverse, inverse


def project(raw, grads):
    unit, inverse = unit_normalize(raw)
    radial = jnp.sum(unit * grads, axis=1, keepdims=True)
    return ((grads - unit * radial) * inverse).astype(BF16)


def kernel(
    far,
    img_ref,
    txt_ref,
    tally_ref,
    sharp_ref,
    shift_ref,
    img_out,
    txt_out,
    images,
    pair_own,
    pair_in,
    texts,
    weights,
    img_keep,
    x_send,
    x_recv,
    z_send,
    z_recv,
    last_img_send,
    last_img_recv,
    core_send,
    core_recv,
    txt_keep,
    y_send,
    y_recv,
    h_send,
    h_recv,
    last_send,
    last_recv,
    send_sem,
    recv_sem,
):
    rows, width = img_ref.shape
    half = rows // 2
    piece = half // PIECES
    pieces = [slice(p * piece, (p + 1) * piece) for p in range(PIECES)]
    loop = lax.axis_index("loop")
    group = lax.axis_index("group")
    x, core = loop // 2, loop % 2
    h, z, y = group // 4, (group // 2) % 2, group % 2

    x_peer = (2 * (1 - x) + core, group)
    core_peer = (2 * x + 1 - core, group)
    z_peer = (loop, 4 * h + 2 * (1 - z) + y)
    y_peer = (loop, 4 * h + 2 * z + 1 - y)

    def h_peer(j):
        return (loop, 4 * ((h + j) % far) + 2 * z + y)

    barrier = pltpu.get_barrier_semaphore()
    peers = [x_peer, core_peer, z_peer, y_peer] + [h_peer(j) for j in range(1, far)]
    for peer in peers:
        pl.semaphore_signal(barrier, inc=1, device_id=peer, device_id_type=MESH)

    started = []

    def start(src, dst, peer):
        index = len(started)
        copy = pltpu.make_async_remote_copy(
            src_ref=src,
            dst_ref=dst,
            send_sem=send_sem.at[index],
            recv_sem=recv_sem.at[index],
            device_id=peer,
            device_id_type=MESH,
        )
        copy.start()
        started.append(copy)
        return copy

    own, beside = 2 * x + z, 2 * x + 1 - z
    across, corner = 2 * (1 - x) + z, 2 * (1 - x) + 1 - z

    txt_unit, _ = unit_normalize(txt_ref[...])
    pair_own[...] = txt_unit.astype(BF16)
    pl.semaphore_wait(barrier, len(peers))
    pair_second = []
    for p in range(PIECES):
        part = pl.ds(half + p * piece, piece)
        pair_second.append(start(pair_own.at[part], pair_in.at[part], y_peer))
    part = pl.ds(0, half)
    pair_first = start(pair_own.at[part], pair_in.at[part], y_peer)
    img_unit, _ = unit_normalize(img_ref[...])
    images[own] = img_unit.astype(BF16)
    x_copy = start(images.at[own], images.at[own], x_peer)
    z_copy = start(images.at[own], images.at[own], z_peer)

    device = loop * (4 * far) + group
    tally_own = tally_ref[device]
    tally_peer = tally_ref[loop * (4 * far) + 4 * h + 2 * z + 1 - y]
    has_own = jnp.minimum(tally_own, 1).astype(F32)
    has_peer = jnp.minimum(tally_peer, 1).astype(F32)

    far_copies = []
    for p in range(PIECES):
        pair_second[p].wait_recv()
        mine = pair_own[pieces[p]].astype(F32)
        other = pair_in[half + p * piece : half + (p + 1) * piece].astype(F32)
        texts[h, core, y, pieces[p]] = (mine * has_own + other * (1.0 - has_own)).astype(BF16)
        slot = texts.at[h, core, y, pl.ds(p * piece, piece)]
        far_copies.append([start(slot, slot, h_peer(j)) for j in range(1, far)])
    pair_first.wait_recv()
    texts[h, core, 1 - y] = (
        pair_in[:half].astype(F32) * has_peer + pair_own[half:].astype(F32) * (1.0 - has_peer)
    ).astype(BF16)
    core_copies = [start(texts.at[h, core], texts.at[h, core], core_peer)]
    y_forwards = []

    def forward_piece(p):
        copies = []
        for j in range(1, far):
            far_copies[p][j - 1].wait_recv()
            slot = texts.at[(h + far - j) % far, core, y, pl.ds(p * piece, piece)]
            copies.append(start(slot, slot, y_peer))
        y_forwards.append(copies)

    sharpness = sharp_ref[0]
    shift = shift_ref[0]
    row_ids = lax.broadcasted_iota(jnp.int32, (rows, 1), 0)

    def weigh(place, block_texts, diagonal=False):
        sx, sz = place // 2, place % 2
        tally = tally_ref[(2 * sx + core) * (4 * far) + 4 * h + 2 * sz + y]
        scale = jnp.where(row_ids < tally, sharpness, 0.0)
        logits = (
            lax.dot_general(
                images[place], block_texts, (((1,), (1,)), ((), ())), preferred_element_type=F32
            )
            * sharpness
            + shift
        )
        pulled = 1.0 / (1.0 + jnp.exp(-logits))
        if diagonal:
            goal = jnp.where(row_ids < half, y * half, (1 - y) * half - half)
            goal = goal + core * rows + row_ids
            columns = lax.broadcasted_iota(jnp.int32, logits.shape, 1)
            pulled = pulled - jnp.where(columns == goal, 1.0, 0.0)
        weight = (scale * pulled).astype(BF16)
        for c in range(2):
            weights[c, pl.ds(pl.multiple_of(place * rows, rows), rows)] = weight[
                :, c * rows : (c + 1) * rows
            ]
        return weight

    def text_grads(c):
        return lax.dot_general(
            weights[c],
            images[...].reshape(4 * rows, width),
            (((0,), (0,)), ((), ())),
            preferred_element_type=F32,
        ).reshape(2, half, width)

    def send_core(j):
        core_send[j] = text_grads(1 - core)
        copy = start(core_send.at[j], core_recv.at[j], core_peer)
        txt_keep[j] = text_grads(core)
        return copy

    def send_y(j, copy):
        copy.wait_recv()
        y_send[j] = (txt_keep[j, 1 - y] + core_recv[j, 1 - y]).astype(BF16)
        copies = []
        for p in range(PIECES):
            part = pl.ds(p * piece, piece)
            copies.append(start(y_send.at[j, part], y_recv.at[j, part], y_peer))
        txt_keep[j, y] = txt_keep[j, y] + core_recv[j, y]
        return copies

    forward_piece(0)
    x_copy.wait_recv()
    part = pl.ds(half, half)
    corner_b = start(images.at[across, part], images.at[across, part], z_peer)
    z_copy.wait_recv()
    part = pl.ds(0, half)
    corner_a = start(images.at[beside, part], images.at[beside, part], x_peer)

    core_copies[0].wait_recv()

    def near_step(place, diagonal=False):
        block_texts = texts[h].reshape(2 * rows, width)
        weight = weigh(place, block_texts, diagonal)
        img_keep[place] = jnp.dot(weight, block_texts, preferred_element_type=F32)

    near_step(own, True)
    near_step(across)
    near_step(beside)
    for p in range(1, PIECES):
        forward_piece(p)
    corner_a.wait_recv()
    corner_b.wait_recv()
    near_step(corner)
    core_sums = [send_core(0)]
    y_sums = []

    for j in range(1, far):
        for p in range(PIECES):
            y_forwards[p][j - 1].wait_recv()
        pair = texts.at[(h + far - j) % far, core]
        core_copies.append(start(pair, pair, core_peer))
    for j in range(1, far):
        y_sums.append(send_y(j - 1, core_sums[j - 1]))
        core_copies[j].wait_recv()
        block_texts = texts[(h + far - j) % far].reshape(2 * rows, width)
        for place in (corner, across, beside, own):
            weigh(place, block_texts)
        core_sums.append(send_core(j))
        if j < far - 1:
            for place in (corner, across, beside, own):
                row_range = pl.ds(pl.multiple_of(place * rows, rows), rows)
                for c in range(2):
                    img_keep[place] += jnp.dot(
                        weights[c, row_range],
                        texts[(h + far - j) % far, c].reshape(rows, width),
                        preferred_element_type=F32,
                    )

    def last_step(place):
        row_range = pl.ds(pl.multiple_of(place * rows, rows), rows)
        weight = jnp.concatenate([weights[0, row_range], weights[1, row_range]], axis=1)
        block_texts = texts[(h + 1) % far].reshape(2 * rows, width)
        return img_keep[place] + jnp.dot(weight, block_texts, preferred_element_type=F32)

    total = last_step(corner)
    x_send[1 - z] = total[:half].astype(BF16)
    z_send[1 - x] = total[half:].astype(BF16)
    x_first = [start(x_send.at[1 - z], x_recv.at[1 - z], x_peer)]
    z_first = [start(z_send.at[1 - x], z_recv.at[1 - x], z_peer)]
    total = last_step(across)
    x_send[z] = total[:half].astype(BF16)
    x_first.append(start(x_send.at[z], x_recv.at[z], x_peer))
    img_keep[across] = total
    total = last_step(beside)
    z_send[x] = total[half:].astype(BF16)
    z_first.append(start(z_send.at[x], z_recv.at[x], z_peer))
    img_keep[beside] = total

    y_sums.append(send_y(far - 1, core_sums[far - 1]))
    img_keep[own] = last_step(own)

    h_copies = [[None] * far for _ in range(PIECES)]
    for j in range(1, far):
        for p in range(PIECES):
            y_sums[j][p].wait_recv()
            part = pl.ds(p * piece, piece)
            h_send[j, pieces[p]] = (
                txt_keep[j, y, pieces[p]] + y_recv[j, pieces[p]].astype(F32)
            ).astype(BF16)
            h_copies[p][j] = start(h_send.at[j, part], h_recv.at[j, part], h_peer(far - j))

    x_first[0].wait_recv()
    last_img_send[0] = (img_keep[beside, :half] + x_recv[1 - z].astype(F32)).astype(BF16)
    last_z = start(last_img_send.at[0], last_img_recv.at[0], z_peer)
    z_first[0].wait_recv()
    last_img_send[1] = (img_keep[across, half:] + z_recv[1 - x].astype(F32)).astype(BF16)
    last_x = start(last_img_send.at[1], last_img_recv.at[1], x_peer)

    for p in range(PIECES):
        y_sums[0][p].wait_recv()
    last_copies = []
    for p in range(PIECES):
        slot_sum = txt_keep[0, y, pieces[p]] + y_recv[0, pieces[p]].astype(F32)
        for j in range(1, far):
            h_copies[p][j].wait_recv()
            slot_sum = slot_sum + h_recv[j, pieces[p]].astype(F32)
        last_send[pieces[p]] = slot_sum.astype(BF16)
        part = pl.ds(p * piece, piece)
        last_copies.append(start(last_send.at[part], last_recv.at[part], y_peer))
        txt_out[pieces[p]] = project(txt_ref[pieces[p]], slot_sum * has_own)

    x_first[1].wait_recv()
    last_z.wait_recv()
    img_sum = img_keep[own, :half] + x_recv[z].astype(F32) + last_img_recv[0].astype(F32)
    img_out[:half] = project(img_ref[:half], img_sum)
    z_first[1].wait_recv()
    last_x.wait_recv()
    img_sum = img_keep[own, half:] + z_recv[x].astype(F32) + last_img_recv[1].astype(F32)
    img_out[half:] = project(img_ref[half:], img_sum)

    for p in range(PIECES):
        last_copies[p].wait_recv()
        part = slice(half + p * piece, half + (p + 1) * piece)
        txt_out[part] = project(
            txt_ref[part], last_recv[pieces[p]].astype(F32) * (1.0 - has_peer)
        )

    for copy in started:
        copy.wait_send()


def per_device(far, pictures, captions, tally, sharpness, shift):
    rows, width = pictures.shape
    half = rows // 2
    vmem = pl.BlockSpec(memory_space=pltpu.VMEM)
    smem = pl.BlockSpec(memory_space=pltpu.SMEM)
    shape = jax.ShapeDtypeStruct((rows, width), BF16)
    copies = 16 + 4 * PIECES + far * (2 + 4 * PIECES)

    def scratch(*sizes, dtype=BF16):
        return pltpu.VMEM((*sizes, width), dtype)

    return pl.pallas_call(
        functools.partial(kernel, far),
        out_shape=(shape, shape),
        in_specs=[vmem, vmem, smem, smem, smem],
        out_specs=(vmem, vmem),
        scratch_shapes=[
            scratch(4, rows),
            scratch(rows),
            scratch(rows),
            scratch(far, 2, 2, half),
            pltpu.VMEM((2, 4 * rows, rows), BF16),
            scratch(4, rows, dtype=F32),
            scratch(2, half),
            scratch(2, half),
            scratch(2, half),
            scratch(2, half),
            scratch(2, half),
            scratch(2, half),
            scratch(far, 2, half, dtype=F32),
            scratch(far, 2, half, dtype=F32),
            scratch(far, 2, half, dtype=F32),
            scratch(far, half),
            scratch(far, half),
            scratch(far, half),
            scratch(far, half),
            scratch(half),
            scratch(half),
            pltpu.SemaphoreType.DMA((copies,)),
            pltpu.SemaphoreType.DMA((copies,)),
        ],
        compiler_params=pltpu.CompilerParams(
            collective_id=0, has_side_effects=True, vmem_limit_bytes=60 * 1024 * 1024
        ),
    )(pictures, captions, tally, sharpness, shift)


def solution(mesh):
    far = mesh.shape["group"] // 4
    spec = P(("loop", "group"), None)
    return jax.shard_map(
        functools.partial(per_device, far),
        mesh=mesh,
        in_specs=(spec, spec, P(), P(), P()),
        out_specs=(spec, spec),
        check_vma=False,
    )
```

time: 64.3 us -> 48.5 us (0.75)
  the two profiles are of different devices: /device:TPU:8 before, /device:TPU:0 now
where the time goes in v2:
time: 48.5 us; the launch traced here: 48.3 us
  Pallas kernels  43.9 us (91%)
  local copies, waits for them, and re-layouts  2.46 us (5%)
  between operations  1.94 us (4%)
    pallas_call x1, Pallas kernels, per_device(): pl.pallas_call(functools.partial(kernel, far), out_shape=(shape, shape),...  43.9 us
    unnamed x4, local copies, waits for them, and re-layouts  2.46 us

profile of v2, /device:TPU:0, one launch (start us, length us, event | category | flops | bytes accessed | tf_op | source)
XLA Modules:
  0.0 48.3 jit_solution(13408937285600710838)
XLA Ops:
  1.9 43.9 %shard_map.68 = (bf16[128,1152]{1,0:T(8,128)(2,1)}, bf16[128,1152]{1,0:T(8,128)(2,1)}) custom-call(bf16[128,1152]{1,0:T(8,128)(2,1)} %img_ref.1, bf16[128,1152]{1,0:T(8,128)(2,1)} %txt_ref.1, s32[32]{0:T(128)} %tally_ref.1, f32[1]{0:T(128)S(6)} %copy.9.sharp_ref, f32[1]{0:T(128)S(6)} %copy.10.shift_ref), custom_call_target="tpu_custom_call" | custom-call | tf_op jit(solution)/shard_map/pallas_call | solution.py:329
  45.8 0.0 copy-start
  45.8 1.7 %copy.11 = bf16[128,1152]{1,0:T(8,128)(2,1)} copy(bf16[128,1152]{1,0:T(8,128)(2,1)} %get-tuple-element.4) | data formatting | bytes 589824
  47.6 0.0 copy-done
  47.6 0.7 %copy.12 = bf16[128,1152]{1,0:T(8,128)(2,1)} copy(bf16[128,1152]{1,0:T(8,128)(2,1)S(1)} %copy-done) | data formatting | bytes 589824
Async XLA Ops:
  45.8 1.8 %copy-start = (bf16[128,1152]{1,0:T(8,128)(2,1)S(1)}, bf16[128,1152]{1,0:T(8,128)(2,1)}, u32[]{:S(2)}) copy-start(bf16[128,1152]{1,0:T(8,128)(2,1)} %get-tuple-element.5) | copy-start | bytes 884740

commit v3 on v2

--- a/solution.py
+++ b/solution.py
@@ -44,8 +44,10 @@
     x_recv,
     z_send,
     z_recv,
-    last_img_send,
-    last_img_recv,
+    low_send,
+    low_recv,
+    high_send,
+    high_recv,
     core_send,
     core_recv,
     txt_keep,
@@ -60,6 +62,7 @@
 ):
     rows, width = img_ref.shape
     half = rows // 2
+    cut = rows * 3 // 4
     piece = half // PIECES
     pieces = [slice(p * piece, (p + 1) * piece) for p in range(PIECES)]
     loop = lax.axis_index("loop")
@@ -110,8 +113,14 @@
     pair_first = start(pair_own.at[part], pair_in.at[part], y_peer)
     img_unit, _ = unit_normalize(img_ref[...])
     images[own] = img_unit.astype(BF16)
-    x_copy = start(images.at[own], images.at[own], x_peer)
-    z_copy = start(images.at[own], images.at[own], z_peer)
+    low, high = pl.ds(0, cut), pl.ds(cut, rows - cut)
+
+    def send_image(place, part, peer):
+        return start(images.at[place, part], images.at[place, part], peer)
+
+    x_high = send_image(own, high, x_peer)
+    z_low = send_image(own, low, z_peer)
+    x_low = send_image(own, low, x_peer)
 
     device = loop * (4 * far) + group
     tally_own = tally_ref[device]
@@ -127,6 +136,9 @@
         texts[h, core, y, pieces[p]] = (mine * has_own + other * (1.0 - has_own)).astype(BF16)
         slot = texts.at[h, core, y, pl.ds(p * piece, piece)]
         far_copies.append([start(slot, slot, h_peer(j)) for j in range(1, far)])
+    z_high = send_image(own, high, z_peer)
+    x_high.wait_recv()
+    corner_high = send_image(across, high, z_peer)
     pair_first.wait_recv()
     texts[h, core, 1 - y] = (
         pair_in[:half].astype(F32) * has_peer + pair_own[half:].astype(F32) * (1.0 - has_peer)
@@ -194,13 +206,8 @@
         txt_keep[j, y] = txt_keep[j, y] + core_recv[j, y]
         return copies
 
-    forward_piece(0)
-    x_copy.wait_recv()
-    part = pl.ds(half, half)
-    corner_b = start(images.at[across, part], images.at[across, part], z_peer)
-    z_copy.wait_recv()
-    part = pl.ds(0, half)
-    corner_a = start(images.at[beside, part], images.at[beside, part], x_peer)
+    z_low.wait_recv()
+    corner_low = send_image(beside, low, x_peer)
 
     core_copies[0].wait_recv()
 
@@ -210,12 +217,15 @@
         img_keep[place] = jnp.dot(weight, block_texts, preferred_element_type=F32)
 
     near_step(own, True)
+    forward_piece(0)
+    x_low.wait_recv()
     near_step(across)
-    near_step(beside)
     for p in range(1, PIECES):
         forward_piece(p)
-    corner_a.wait_recv()
-    corner_b.wait_recv()
+    z_high.wait_recv()
+    near_step(beside)
+    corner_low.wait_recv()
+    corner_high.wait_recv()
     near_step(corner)
     core_sums = [send_core(0)]
     y_sums = []
@@ -225,45 +235,47 @@
             y_forwards[p][j - 1].wait_recv()
         pair = texts.at[(h + far - j) % far, core]
         core_copies.append(start(pair, pair, core_peer))
-    for j in range(1, far):
+    for j in range(1, far - 1):
         y_sums.append(send_y(j - 1, core_sums[j - 1]))
         core_copies[j].wait_recv()
         block_texts = texts[(h + far - j) % far].reshape(2 * rows, width)
         for place in (corner, across, beside, own):
-            weigh(place, block_texts)
+            weight = weigh(place, block_texts)
+            img_keep[place] += jnp.dot(weight, block_texts, preferred_element_type=F32)
         core_sums.append(send_core(j))
-        if j < far - 1:
-            for place in (corner, across, beside, own):
-                row_range = pl.ds(pl.multiple_of(place * rows, rows), rows)
-                for c in range(2):
-                    img_keep[place] += jnp.dot(
-                        weights[c, row_range],
-                        texts[(h + far - j) % far, c].reshape(rows, width),
-                        preferred_element_type=F32,
-                    )
-
-    def last_step(place):
+
+    y_sums.append(send_y(far - 2, core_sums[far - 2]))
+    core_copies[far - 1].wait_recv()
+
+    def last_texts():
+        return texts[(h + 1) % far].reshape(2 * rows, width)
+
+    def last_step(place, weight):
+        return img_keep[place] + jnp.dot(weight, last_texts(), preferred_element_type=F32)
+
+    def stored(place):
         row_range = pl.ds(pl.multiple_of(place * rows, rows), rows)
-        weight = jnp.concatenate([weights[0, row_range], weights[1, row_range]], axis=1)
-        block_texts = texts[(h + 1) % far].reshape(2 * rows, width)
-        return img_keep[place] + jnp.dot(weight, block_texts, preferred_element_type=F32)
-
-    total = last_step(corner)
-    x_send[1 - z] = total[:half].astype(BF16)
-    z_send[1 - x] = total[half:].astype(BF16)
+        return jnp.concatenate([weights[0, row_range], weights[1, row_range]], axis=1)
+
+    total = last_step(corner, weigh(corner, last_texts()))
+    x_send[1 - z] = total[:cut].astype(BF16)
     x_first = [start(x_send.at[1 - z], x_recv.at[1 - z], x_peer)]
+    z_send[1 - x] = total[cut:].astype(BF16)
     z_first = [start(z_send.at[1 - x], z_recv.at[1 - x], z_peer)]
-    total = last_step(across)
-    x_send[z] = total[:half].astype(BF16)
+    for place in (across, beside, own):
+        weigh(place, last_texts())
+    core_sums.append(send_core(far - 1))
+    total = last_step(across, stored(across))
+    x_send[z] = total[:cut].astype(BF16)
     x_first.append(start(x_send.at[z], x_recv.at[z], x_peer))
     img_keep[across] = total
-    total = last_step(beside)
-    z_send[x] = total[half:].astype(BF16)
+    total = last_step(beside, stored(beside))
+    z_send[x] = total[cut:].astype(BF16)
     z_first.append(start(z_send.at[x], z_recv.at[x], z_peer))
     img_keep[beside] = total
 
     y_sums.append(send_y(far - 1, core_sums[far - 1]))
-    img_keep[own] = last_step(own)
+    img_keep[own] = last_step(own, stored(own))
 
     h_copies = [[None] * far for _ in range(PIECES)]
     for j in range(1, far):
@@ -275,12 +287,12 @@
             ).astype(BF16)
             h_copies[p][j] = start(h_send.at[j, part], h_recv.at[j, part], h_peer(far - j))
 
+    z_first[0].wait_recv()
+    high_send[...] = (img_keep[across, cut:] + z_recv[1 - x].astype(F32)).astype(BF16)
+    last_x = start(high_send, high_recv, x_peer)
     x_first[0].wait_recv()
-    last_img_send[0] = (img_keep[beside, :half] + x_recv[1 - z].astype(F32)).astype(BF16)
-    last_z = start(last_img_send.at[0], last_img_recv.at[0], z_peer)
-    z_first[0].wait_recv()
-    last_img_send[1] = (img_keep[across, half:] + z_recv[1 - x].astype(F32)).astype(BF16)
-    last_x = start(last_img_send.at[1], last_img_recv.at[1], x_peer)
+    low_send[...] = (img_keep[beside, :cut] + x_recv[1 - z].astype(F32)).astype(BF16)
+    last_z = start(low_send, low_recv, z_peer)
 
     for p in range(PIECES):
         y_sums[0][p].wait_recv()
@@ -295,14 +307,14 @@
         last_copies.append(start(last_send.at[part], last_recv.at[part], y_peer))
         txt_out[pieces[p]] = project(txt_ref[pieces[p]], slot_sum * has_own)
 
+    z_first[1].wait_recv()
+    last_x.wait_recv()
+    img_sum = img_keep[own, cut:] + z_recv[x].astype(F32) + high_recv[...].astype(F32)
+    img_out[cut:] = project(img_ref[cut:], img_sum)
     x_first[1].wait_recv()
     last_z.wait_recv()
-    img_sum = img_keep[own, :half] + x_recv[z].astype(F32) + last_img_recv[0].astype(F32)
-    img_out[:half] = project(img_ref[:half], img_sum)
-    z_first[1].wait_recv()
-    last_x.wait_recv()
-    img_sum = img_keep[own, half:] + z_recv[x].astype(F32) + last_img_recv[1].astype(F32)
-    img_out[half:] = project(img_ref[half:], img_sum)
+    img_sum = img_keep[own, :cut] + x_recv[z].astype(F32) + low_recv[...].astype(F32)
+    img_out[:cut] = project(img_ref[:cut], img_sum)
 
     for p in range(PIECES):
         last_copies[p].wait_recv()
@@ -318,6 +330,7 @@
 def per_device(far, pictures, captions, tally, sharpness, shift):
     rows, width = pictures.shape
     half = rows // 2
+    cut = rows * 3 // 4
     vmem = pl.BlockSpec(memory_space=pltpu.VMEM)
     smem = pl.BlockSpec(memory_space=pltpu.SMEM)
     shape = jax.ShapeDtypeStruct((rows, width), BF16)
@@ -338,12 +351,14 @@
             scratch(far, 2, 2, half),
             pltpu.VMEM((2, 4 * rows, rows), BF16),
             scratch(4, rows, dtype=F32),
-            scratch(2, half),
-            scratch(2, half),
-            scratch(2, half),
-            scratch(2, half),
-            scratch(2, half),
-            scratch(2, half),
+            scratch(2, cut),
+            scratch(2, cut),
+            scratch(2, rows - cut),
+            scratch(2, rows - cut),
+            scratch(cut),
+            scratch(cut),
+            scratch(rows - cut),
+            scratch(rows - cut),
             scratch(far, 2, half, dtype=F32),
             scratch(far, 2, half, dtype=F32),
             scratch(far, 2, half, dtype=F32),

time: 48.5 us -> 47.2 us (0.973)
  Pallas kernels: 43.9 us -> 42.6 us
    pallas_call x1, Pallas kernels: 43.9 us -> 42.6 us  [per_device(): pl.pallas_call(functools.partial(kernel, far), out_shape=(shape, shape),...]
where the time goes in v3:
time: 47.2 us; the launch traced here: 47 us
  Pallas kernels  42.6 us (90%)
  local copies, waits for them, and re-layouts  2.46 us (5%)
  between operations  1.94 us (4%)
    pallas_call x1, Pallas kernels, per_device(): pl.pallas_call(functools.partial(kernel, far), out_shape=(shape, shape),...  42.6 us
    unnamed x4, local copies, waits for them, and re-layouts  2.46 us

profile of v3, /device:TPU:0, one launch (start us, length us, event | category | flops | bytes accessed | tf_op | source)
XLA Modules:
  0.0 47.0 jit_solution(6290809422928010331)
XLA Ops:
  1.9 42.6 %shard_map.68 = (bf16[128,1152]{1,0:T(8,128)(2,1)}, bf16[128,1152]{1,0:T(8,128)(2,1)}) custom-call(bf16[128,1152]{1,0:T(8,128)(2,1)} %img_ref.1, bf16[128,1152]{1,0:T(8,128)(2,1)} %txt_ref.1, s32[32]{0:T(128)} %tally_ref.1, f32[1]{0:T(128)S(6)} %copy.9.sharp_ref, f32[1]{0:T(128)S(6)} %copy.10.shift_ref), custom_call_target="tpu_custom_call" | custom-call | tf_op jit(solution)/shard_map/pallas_call | solution.py:342
  44.5 0.0 copy-start
  44.5 1.7 %copy.11 = bf16[128,1152]{1,0:T(8,128)(2,1)} copy(bf16[128,1152]{1,0:T(8,128)(2,1)} %get-tuple-element.4) | data formatting | bytes 589824
  46.3 0.0 copy-done
  46.3 0.7 %copy.12 = bf16[128,1152]{1,0:T(8,128)(2,1)} copy(bf16[128,1152]{1,0:T(8,128)(2,1)S(1)} %copy-done) | data formatting | bytes 589824
Async XLA Ops:
  44.5 1.8 %copy-start = (bf16[128,1152]{1,0:T(8,128)(2,1)S(1)}, bf16[128,1152]{1,0:T(8,128)(2,1)}, u32[]{:S(2)}) copy-start(bf16[128,1152]{1,0:T(8,128)(2,1)} %get-tuple-element.5) | copy-start | bytes 884740

commit v4 on v3

--- a/solution.py
+++ b/solution.py
@@ -10,7 +10,7 @@
 MESH = pl.DeviceIdType.MESH
 F32 = jnp.float32
 BF16 = jnp.bfloat16
-PIECES = 2
+PIECES = 4
 
 
 def unit_normalize(raw):
@@ -62,7 +62,7 @@
 ):
     rows, width = img_ref.shape
     half = rows // 2
-    cut = rows * 3 // 4
+    cut = rows * 5 // 8
     piece = half // PIECES
     pieces = [slice(p * piece, (p + 1) * piece) for p in range(PIECES)]
     loop = lax.axis_index("loop")
@@ -330,7 +330,7 @@
 def per_device(far, pictures, captions, tally, sharpness, shift):
     rows, width = pictures.shape
     half = rows // 2
-    cut = rows * 3 // 4
+    cut = rows * 5 // 8
     vmem = pl.BlockSpec(memory_space=pltpu.VMEM)
     smem = pl.BlockSpec(memory_space=pltpu.SMEM)
     shape = jax.ShapeDtypeStruct((rows, width), BF16)
@@ -372,7 +372,7 @@
             pltpu.SemaphoreType.DMA((copies,)),
         ],
         compiler_params=pltpu.CompilerParams(
-            collective_id=0, has_side_effects=True, vmem_limit_bytes=60 * 1024 * 1024
+            collective_id=0, has_side_effects=True, vmem_limit_bytes=(16 + 8 * far) << 20
         ),
     )(pictures, captions, tally, sharpness, shift)
 

time: 47.2 us -> 46 us (0.975)
  Pallas kernels: 42.6 us -> 40.4 us
  local copies, waits for them, and re-layouts: 2.46 us -> 3.35 us
    pallas_call x1, Pallas kernels: 42.6 us -> 40.4 us  [per_device(): pl.pallas_call(functools.partial(kernel, far), out_shape=(shape, shape),...]
    unnamed x4 -> x8, local copies, waits for them, and re-layouts: 2.46 us -> 3.35 us
where the time goes in v4:
time: 46 us; the launch traced here: 45.8 us
  Pallas kernels  40.4 us (88%)
  local copies, waits for them, and re-layouts  3.35 us (7%)
  between operations  1.97 us (4%)
    pallas_call x1, Pallas kernels, per_device(): pl.pallas_call(functools.partial(kernel, far), out_shape=(shape, shape),...  40.4 us
    unnamed x8, local copies, waits for them, and re-layouts  3.35 us

profile of v4, /device:TPU:0, one launch (start us, length us, event | category | flops | bytes accessed | tf_op | source)
XLA Modules:
  0.0 45.8 jit_solution(13713759368730451083)
XLA Ops:
  1.3 0.0 copy-start.2
  1.9 0.0 copy-done.2
  2.0 0.0 copy-start
  2.0 1.0 %copy-done = bf16[128,1152]{1,0:T(8,128)(2,1)S(1)} copy-done((bf16[128,1152]{1,0:T(8,128)(2,1)S(1)}, bf16[128,1152]{1,0:T(8,128)(2,1)}, u32[]{:S(2)}) %copy-start) | copy-done | bytes 294936
  2.9 0.0 copy-start.1
  2.9 1.0 %copy-done.1 = bf16[128,1152]{1,0:T(8,128)(2,1)S(1)} copy-done((bf16[128,1152]{1,0:T(8,128)(2,1)S(1)}, bf16[128,1152]{1,0:T(8,128)(2,1)}, u32[]{:S(2)}) %copy-start.1) | copy-done | bytes 294936
  3.9 40.4 %shard_map.68 = (bf16[128,1152]{1,0:T(8,128)(2,1)S(1)}, bf16[128,1152]{1,0:T(8,128)(2,1)S(1)}) custom-call(bf16[128,1152]{1,0:T(8,128)(2,1)S(1)} %copy-done, bf16[128,1152]{1,0:T(8,128)(2,1)S(1)} %copy-done.1, s32[32]{0:T(128)S(1)} %copy-done.2, f32[1]{0:T(128)S(6)} %copy.9.sharp_ref, f32[1]{0:T(128)S(6)} %copy.10.shift_ref), custom_call_target="tpu_custom_call" | custom-call | tf_op jit(solution)/shard_map/pallas_call | solution.py:342
  44.3 0.7 %copy.11 = bf16[128,1152]{1,0:T(8,128)(2,1)} copy(bf16[128,1152]{1,0:T(8,128)(2,1)S(1)} %get-tuple-element.4) | data formatting | bytes 589824
  45.1 0.7 %copy.12 = bf16[128,1152]{1,0:T(8,128)(2,1)} copy(bf16[128,1152]{1,0:T(8,128)(2,1)S(1)} %get-tuple-element.5) | data formatting | bytes 589824
Async XLA Ops:
  1.3 0.7 %copy-start.2 = (s32[32]{0:T(128)S(1)}, s32[32]{0:T(128)}, u32[]{:S(2)}) copy-start(s32[32]{0:T(128)} %tally_ref.1) | copy-start | bytes 388
  2.0 1.0 %copy-start = (bf16[128,1152]{1,0:T(8,128)(2,1)S(1)}, bf16[128,1152]{1,0:T(8,128)(2,1)}, u32[]{:S(2)}) copy-start(bf16[128,1152]{1,0:T(8,128)(2,1)} %img_ref.1) | copy-start | bytes 884740
  2.9 1.0 %copy-start.1 = (bf16[128,1152]{1,0:T(8,128)(2,1)S(1)}, bf16[128,1152]{1,0:T(8,128)(2,1)}, u32[]{:S(2)}) copy-start(bf16[128,1152]{1,0:T(8,128)(2,1)} %txt_ref.1) | copy-start | bytes 884740

commit v5 on v4

--- a/solution.py
+++ b/solution.py
@@ -257,14 +257,14 @@
         row_range = pl.ds(pl.multiple_of(place * rows, rows), rows)
         return jnp.concatenate([weights[0, row_range], weights[1, row_range]], axis=1)
 
-    total = last_step(corner, weigh(corner, last_texts()))
+    for place in (corner, across, beside, own):
+        weigh(place, last_texts())
+    core_sums.append(send_core(far - 1))
+    total = last_step(corner, stored(corner))
     x_send[1 - z] = total[:cut].astype(BF16)
     x_first = [start(x_send.at[1 - z], x_recv.at[1 - z], x_peer)]
     z_send[1 - x] = total[cut:].astype(BF16)
     z_first = [start(z_send.at[1 - x], z_recv.at[1 - x], z_peer)]
-    for place in (across, beside, own):
-        weigh(place, last_texts())
-    core_sums.append(send_core(far - 1))
     total = last_step(across, stored(across))
     x_send[z] = total[:cut].astype(BF16)
     x_first.append(start(x_send.at[z], x_recv.at[z], x_peer))

time: 46 us -> 46 us (level)
  no operation moved by 1% of the time
where the time goes in v5:
time: 46 us; the launch traced here: 45.8 us
  Pallas kernels  40.5 us (88%)
  local copies, waits for them, and re-layouts  3.35 us (7%)
  between operations  1.97 us (4%)
    pallas_call x1, Pallas kernels, per_device(): pl.pallas_call(functools.partial(kernel, far), out_shape=(shape, shape),...  40.5 us
    unnamed x8, local copies, waits for them, and re-layouts  3.35 us

profile of v5, /device:TPU:0, one launch (start us, length us, event | category | flops | bytes accessed | tf_op | source)
XLA Modules:
  0.0 45.8 jit_solution(16941136348287682760)
XLA Ops:
  1.3 0.0 copy-start.2
  1.9 0.0 copy-done.2
  2.0 0.0 copy-start
  2.0 1.0 %copy-done = bf16[128,1152]{1,0:T(8,128)(2,1)S(1)} copy-done((bf16[128,1152]{1,0:T(8,128)(2,1)S(1)}, bf16[128,1152]{1,0:T(8,128)(2,1)}, u32[]{:S(2)}) %copy-start) | copy-done | bytes 294936
  2.9 0.0 copy-start.1
  2.9 1.0 %copy-done.1 = bf16[128,1152]{1,0:T(8,128)(2,1)S(1)} copy-done((bf16[128,1152]{1,0:T(8,128)(2,1)S(1)}, bf16[128,1152]{1,0:T(8,128)(2,1)}, u32[]{:S(2)}) %copy-start.1) | copy-done | bytes 294936
  3.9 40.5 %shard_map.68 = (bf16[128,1152]{1,0:T(8,128)(2,1)S(1)}, bf16[128,1152]{1,0:T(8,128)(2,1)S(1)}) custom-call(bf16[128,1152]{1,0:T(8,128)(2,1)S(1)} %copy-done, bf16[128,1152]{1,0:T(8,128)(2,1)S(1)} %copy-done.1, s32[32]{0:T(128)S(1)} %copy-done.2, f32[1]{0:T(128)S(6)} %copy.9.sharp_ref, f32[1]{0:T(128)S(6)} %copy.10.shift_ref), custom_call_target="tpu_custom_call" | custom-call | tf_op jit(solution)/shard_map/pallas_call | solution.py:342
  44.4 0.7 %copy.11 = bf16[128,1152]{1,0:T(8,128)(2,1)} copy(bf16[128,1152]{1,0:T(8,128)(2,1)S(1)} %get-tuple-element.4) | data formatting | bytes 589824
  45.1 0.7 %copy.12 = bf16[128,1152]{1,0:T(8,128)(2,1)} copy(bf16[128,1152]{1,0:T(8,128)(2,1)S(1)} %get-tuple-element.5) | data formatting | bytes 589824
Async XLA Ops:
  1.3 0.7 %copy-start.2 = (s32[32]{0:T(128)S(1)}, s32[32]{0:T(128)}, u32[]{:S(2)}) copy-start(s32[32]{0:T(128)} %tally_ref.1) | copy-start | bytes 388
  2.0 1.0 %copy-start = (bf16[128,1152]{1,0:T(8,128)(2,1)S(1)}, bf16[128,1152]{1,0:T(8,128)(2,1)}, u32[]{:S(2)}) copy-start(bf16[128,1152]{1,0:T(8,128)(2,1)} %img_ref.1) | copy-start | bytes 884740
  2.9 1.0 %copy-start.1 = (bf16[128,1152]{1,0:T(8,128)(2,1)S(1)}, bf16[128,1152]{1,0:T(8,128)(2,1)}, u32[]{:S(2)}) copy-start(bf16[128,1152]{1,0:T(8,128)(2,1)} %txt_ref.1) | copy-start | bytes 884740
